TPU v7x, 32 devices: a whole 2x2x4 slice. The times are simulated.
32 devices in a mesh: dp: 8 (over z, y), pipe: 2 (over x), pair: 2 (over core).
Axes of the slice: x: 2, y: 2, z: 4, core: 2. Of those that a mesh axis runs over, the one named last changes fastest.
Arguments:
- inputs: bfloat16 [7680, 768], P(('dp', 'pair')), may hold values from -6 to 6
- cotangent: bfloat16 [7680, 768], P(('dp', 'pair')), may hold values from -6 to 6
- text_mask: int32 [32, 176], P(('dp', 'pair')), may hold values 0 or 1
- seg_count: int32 [32], P(('dp', 'pair')), may hold values from 5 to 64, as said below
- align: int32 [32, 176], P(('dp', 'pair')), may hold values from 0 to 63, as said below
- w_qkv: bfloat16 [2, 768, 2304], P('pipe', 'pair'), may hold values from -0.21875 to 0.21875
- w_out: bfloat16 [2, 768, 768], P('pipe', 'pair'), may hold values from -0.875 to 0.875
- w_up: bfloat16 [2, 768, 3072], P('pipe', 'pair'), may hold values from -0.21875 to 0.21875
- w_down: bfloat16 [2, 3072, 768], P('pipe', 'pair'), may hold values from -0.109375 to 0.109375
- bias_qv: bfloat16 [2, 2, 768], P('pipe', None, 'pair'), may hold values from -3 to 3
- bias_up: bfloat16 [2, 3072], P('pipe', 'pair'), may hold values from -3 to 3
- bias_res: bfloat16 [2, 2, 768], P('pipe', None, 'pair'), may hold values from -3 to 3
- norm_gain: bfloat16 [2, 2, 768], P('pipe', None, 'pair'), may hold values from 0.5 to 1.5
- norm_shift: bfloat16 [2, 2, 768], P('pipe', None, 'pair'), may hold values from -3 to 3
Outputs:
- section_out: bfloat16 [2, 7680, 768], P('pipe', ('dp', 'pair'))
- input_grad: bfloat16 [2, 7680, 768], P('pipe', ('dp', 'pair'))
- grad_w_qkv: float32 [2, 768, 2304], P('pipe', 'pair')
- grad_w_out: float32 [2, 768, 768], P('pipe', 'pair')
- grad_w_up: float32 [2, 768, 3072], P('pipe', 'pair')
- grad_w_down: float32 [2, 3072, 768], P('pipe', 'pair')
- grad_bias_qv: float32 [2, 2, 768], P('pipe', None, 'pair')
- grad_bias_up: float32 [2, 3072], P('pipe', 'pair')
- grad_bias_res: float32 [2, 2, 768], P('pipe', None, 'pair')
- grad_norm_gain: float32 [2, 2, 768], P('pipe', None, 'pair')
- grad_norm_shift: float32 [2, 2, 768], P('pipe', None, 'pair')
Inputs may be any that keep to these rules, and one draw needn't show every extreme that they name: `seg_count`: heavy-tailed; some document has 64 segments. `align`: each value is below its document's seg_count.
All inputs are finite; a program needn't handle non-finite values. No bound on the sum of `text_mask` on one device may be relied on, other than what follows from the above.
Results may differ from a plain program's by a relative error of at most 0.024.
Values may be sent and summed in bfloat16 or wider, within the bound.
No kernel may reach another device: no remote copies, remote signals or barrier semaphores. Data moves between devices by JAX's collectives and lax.ppermute only.
A program may use at most 192 MiB of HBM per device.

v0:
```python
import jax
import jax.numpy as jnp
from jax import lax
from jax.sharding import PartitionSpec as P

D = 768
HEADS = 12
HEAD = 64
TEXT = 176
SLOTS = 64
SEQ = 240
MB = 2
DOC_MB = 1


epsilon = 1e-06
masked_score = -1e30


def passed_along(block, axis, distance):
    devices = range(lax.axis_size(axis))
    route = [(i - distance, i) for i in devices if i - distance in devices]
    return lax.ppermute(block, axis, route)


def layer_norm(values, gain, shift):
    center = values - jnp.mean(values, axis=-1, keepdims=True)
    spread = jnp.mean(center * center, axis=-1, keepdims=True)
    return center * lax.rsqrt(spread + epsilon) * gain + shift


def build_keep(text_mask, seg_count, align):
    documents = align.shape[0]
    slot_iota = jnp.arange(SLOTS, dtype=jnp.int32)
    key_valid = jnp.concatenate([text_mask == 1, slot_iota[None, :] < seg_count[:, None]], axis=1)
    owned_by = align[:, None, :] == slot_iota[None, :, None]
    slot_rows = jnp.concatenate([owned_by, jnp.ones((documents, SLOTS, SLOTS), dtype=bool)], axis=2)
    text_rows = jnp.ones((documents, TEXT, SEQ), dtype=bool)
    allowed = jnp.concatenate([text_rows, slot_rows], axis=1)
    return allowed & key_valid[:, None, :]


def split_heads(array, documents):
    return array.reshape(documents, SEQ, HEADS, HEAD)


def head_scores(queries, keys_all, keep):
    documents = keep.shape[0]
    scores = jnp.einsum(
        "dqhe,dkhe->dhqk",
        split_heads(queries, documents),
        split_heads(keys_all, documents),
        preferred_element_type=jnp.float32,
    )
    return jnp.where(keep[:, None], scores, masked_score)


def layer_forward(tokens_in, keep, weights):
    w_qkv, w_out, w_up, w_down, bias_qv, bias_up, bias_res, norm_gain, norm_shift = weights
    row_count = tokens_in.shape[0]
    documents = keep.shape[0]
    projected = jnp.dot(tokens_in, w_qkv, preferred_element_type=jnp.float32)
    queries = ((projected[:, :D] + bias_qv[0]) * 0.125).astype(jnp.bfloat16)
    keys_all = projected[:, D : 2 * D].astype(jnp.bfloat16)
    values_all = (projected[:, 2 * D :] + bias_qv[1]).astype(jnp.bfloat16)
    scores = head_scores(queries, keys_all, keep)
    log_total = jax.nn.logsumexp(scores, axis=-1, keepdims=True)
    attention = jnp.exp(scores - log_total).astype(jnp.bfloat16)
    context = jnp.einsum(
        "dhqk,dkhe->dqhe",
        attention,
        split_heads(values_all, documents),
        preferred_element_type=jnp.float32,
    )
    context = context.reshape(row_count, D).astype(jnp.bfloat16)
    summed_one = (
        tokens_in.astype(jnp.float32)
        + jnp.dot(context, w_out, preferred_element_type=jnp.float32)
        + bias_res[0]
    )
    normed = layer_norm(summed_one, norm_gain[0], norm_shift[0])
    normed_low = normed.astype(jnp.bfloat16)
    inner = jnp.dot(normed_low, w_up, preferred_element_type=jnp.float32) + bias_up
    activated = jax.nn.gelu(inner).astype(jnp.bfloat16)
    summed_two = (
        normed + jnp.dot(activated, w_down, preferred_element_type=jnp.float32) + bias_res[1]
    )
    layer_out = layer_norm(summed_two, norm_gain[1], norm_shift[1]).astype(jnp.bfloat16)
    return (
        layer_out,
        (
            tokens_in,
            queries,
            keys_all,
            values_all,
            log_total,
            context,
            summed_one,
            normed_low,
            inner,
            activated,
            summed_two,
        ),
    )


def layer_backward(grad_out, saved, keep, weights):
    w_qkv, w_out, w_up, w_down, bias_qv, bias_up, bias_res, norm_gain, norm_shift = weights
    (
        tokens_in,
        queries,
        keys_all,
        values_all,
        log_total,
        context,
        summed_one,
        normed_low,
        inner,
        activated,
        summed_two,
    ) = saved
    row_count = tokens_in.shape[0]
    documents = keep.shape[0]
    gain_wide = norm_gain.astype(jnp.float32)
    shift_wide = norm_shift.astype(jnp.float32)
    unused, second_back = jax.vjp(layer_norm, summed_two, gain_wide[1], shift_wide[1])
    grad_two, gain_two, shift_two = second_back(grad_out.astype(jnp.float32))
    branch_low = grad_two.astype(jnp.bfloat16)
    grad_active = jnp.einsum("rd,fd->rf", branch_low, w_down, preferred_element_type=jnp.float32)
    unused, gelu_back = jax.vjp(jax.nn.gelu, inner)
    inner_low = gelu_back(grad_active)[0].astype(jnp.bfloat16)
    grad_normed = grad_two + jnp.einsum(
        "rf,df->rd", inner_low, w_up, preferred_element_type=jnp.float32
    )
    unused, first_back = jax.vjp(layer_norm, summed_one, gain_wide[0], shift_wide[0])
    grad_one, gain_one, shift_one = first_back(grad_normed)
    attend_low = grad_one.astype(jnp.bfloat16)
    context_low = jnp.einsum(
        "rd,cd->rc", attend_low, w_out, preferred_element_type=jnp.float32
    ).astype(jnp.bfloat16)
    scores = head_scores(queries, keys_all, keep)
    attention_wide = jnp.exp(scores - log_total)
    attention = attention_wide.astype(jnp.bfloat16)
    context_heads = split_heads(context_low, documents)
    grad_attention = jnp.einsum(
        "dqhe,dkhe->dhqk",
        context_heads,
        split_heads(values_all, documents),
        preferred_element_type=jnp.float32,
    )
    grad_values = jnp.einsum(
        "dhqk,dqhe->dkhe", attention, context_heads, preferred_element_type=jnp.float32
    )
    grad_values = grad_values.reshape(row_count, D).astype(jnp.bfloat16)
    row_terms = jnp.sum(attention_wide * grad_attention, axis=-1, keepdims=True)
    grad_scores = (attention_wide * (grad_attention - row_terms)).astype(jnp.bfloat16)
    grad_queries = jnp.einsum(
        "dhqk,dkhe->dqhe",
        grad_scores,
        split_heads(keys_all, documents),
        preferred_element_type=jnp.float32,
    )
    grad_queries = grad_queries.reshape(row_count, D).astype(jnp.bfloat16) * 0.125
    grad_keys = jnp.einsum(
        "dhqk,dqhe->dkhe",
        grad_scores,
        split_heads(queries, documents),
        preferred_element_type=jnp.float32,
    )
    grad_keys = grad_keys.reshape(row_count, D).astype(jnp.bfloat16)
    grad_proj = jnp.concatenate([grad_queries, grad_keys, grad_values], axis=1)
    grad_in = (
        grad_one + jnp.einsum("re,de->rd", grad_proj, w_qkv, preferred_element_type=jnp.float32)
    ).astype(jnp.bfloat16)
    grad_gains = jnp.stack([gain_one, gain_two])
    grad_shifts = jnp.stack([shift_one, shift_two])
    factors = (
        tokens_in,
        grad_proj,
        context,
        attend_low,
        normed_low,
        inner_low,
        activated,
        branch_low,
    )
    return (grad_in, (grad_gains, grad_shifts), factors)


def weight_products(factors):
    tokens_in, grad_proj, context, attend_low, normed_low, inner_low, activated, branch_low = (
        factors
    )
    grad_wqkv = jnp.einsum("rd,re->de", tokens_in, grad_proj, preferred_element_type=jnp.float32)
    grad_wout = jnp.einsum("rc,rd->cd", context, attend_low, preferred_element_type=jnp.float32)
    grad_up = jnp.einsum("rd,rf->df", normed_low, inner_low, preferred_element_type=jnp.float32)
    grad_down = jnp.einsum("rf,rd->fd", activated, branch_low, preferred_element_type=jnp.float32)
    proj_sums = jnp.sum(grad_proj.astype(jnp.float32), axis=0)
    grad_bias_qv = jnp.stack([proj_sums[:D], proj_sums[2 * D :]])
    grad_bias_up = jnp.sum(inner_low.astype(jnp.float32), axis=0)
    grad_bias_res = jnp.stack(
        [
            jnp.sum(attend_low.astype(jnp.float32), axis=0),
            jnp.sum(branch_low.astype(jnp.float32), axis=0),
        ]
    )
    return (grad_wqkv, grad_wout, grad_up, grad_down, grad_bias_qv, grad_bias_up, grad_bias_res)


def local(
    inputs,
    cotangent,
    text_mask,
    seg_count,
    align,
    w_qkv,
    w_out,
    w_up,
    w_down,
    bias_qv,
    bias_up,
    bias_res,
    norm_gain,
    norm_shift,
):
    section_index = lax.axis_index("pipe")
    layer_weights = (
        lax.all_gather(w_qkv[0], "pair", axis=0, tiled=True),
        lax.all_gather(w_out[0], "pair", axis=0, tiled=True),
        lax.all_gather(w_up[0], "pair", axis=0, tiled=True),
        lax.all_gather(w_down[0], "pair", axis=0, tiled=True),
        lax.all_gather(bias_qv[0], "pair", axis=1, tiled=True),
        lax.all_gather(bias_up[0], "pair", axis=0, tiled=True),
        lax.all_gather(bias_res[0], "pair", axis=1, tiled=True),
        lax.all_gather(norm_gain[0], "pair", axis=1, tiled=True),
        lax.all_gather(norm_shift[0], "pair", axis=1, tiled=True),
    )
    layer_weights = tuple(layer_weights)
    keep_all = build_keep(text_mask, seg_count, align)
    row_count = DOC_MB * SEQ
    received = jnp.zeros((row_count, D), jnp.bfloat16)
    kept_list = []
    output_list = []
    for moment in range(MB + 1):
        batch_index = jnp.clip(moment - section_index, 0, MB - 1)
        own_rows = lax.dynamic_slice_in_dim(inputs, min(moment, MB - 1) * row_count, row_count, 0)
        layer_in = jnp.where(section_index == 0, own_rows, received)
        keep_now = lax.dynamic_slice_in_dim(keep_all, batch_index * DOC_MB, DOC_MB, 0)
        layer_out, kept = layer_forward(layer_in, keep_now, layer_weights)
        kept_list.append(kept)
        output_list.append(layer_out)
        if moment < MB:
            received = passed_along(layer_out, "pipe", 1)
    kept_stack = jax.tree.map(lambda *leaves: jnp.stack(leaves), *kept_list)
    output_stack = jnp.stack(output_list)
    section_out = jnp.concatenate(
        [
            lax.dynamic_index_in_dim(output_stack, batch_number + section_index, 0, keepdims=False)
            for batch_number in range(MB)
        ],
        axis=0,
    )
    received = jnp.zeros((row_count, D), jnp.bfloat16)
    norm_total = None
    grad_list = []
    factor_list = []
    for moment in range(MB + 1):
        raw_index = MB - moment - section_index
        valid = (raw_index >= 0) & (raw_index < MB)
        batch_index = jnp.clip(raw_index, 0, MB - 1)
        own_grad = lax.dynamic_slice_in_dim(
            cotangent, max(MB - 1 - moment, 0) * row_count, row_count, 0
        )
        grad_now = jnp.where(section_index == 1, own_grad, received)
        grad_now = jnp.where(valid, grad_now, jnp.zeros_like(grad_now))
        saved = jax.tree.map(
            lambda leaf: lax.dynamic_index_in_dim(
                leaf, batch_index + section_index, 0, keepdims=False
            ),
            kept_stack,
        )
        keep_now = lax.dynamic_slice_in_dim(keep_all, batch_index * DOC_MB, DOC_MB, 0)
        grad_in, norm_terms, factors = layer_backward(grad_now, saved, keep_now, layer_weights)
        if norm_total is None:
            norm_total = norm_terms
        else:
            norm_total = jax.tree.map(jnp.add, norm_total, norm_terms)
        grad_list.append(grad_in)
        factor_list.append(factors)
        if moment < MB:
            received = passed_along(grad_in, "pipe", -1)
    grad_stack = jnp.stack(grad_list)
    input_grad = jnp.concatenate(
        [
            lax.dynamic_index_in_dim(
                grad_stack, MB - batch_number - section_index, 0, keepdims=False
            )
            for batch_number in range(MB)
        ],
        axis=0,
    )
    factor_stack = jax.tree.map(lambda *leaves: jnp.stack(leaves), *factor_list)
    first_valid = 1 - section_index
    chosen = jax.tree.map(
        lambda leaf: lax.dynamic_slice_in_dim(leaf, first_valid, MB, 0).reshape(
            (MB * row_count,) + leaf.shape[2:]
        ),
        factor_stack,
    )
    grad_total = weight_products(chosen) + (norm_total[0], norm_total[1])
    shares = (
        lax.psum_scatter(
            grad_total[0].astype(jnp.bfloat16), "pair", scatter_dimension=0, tiled=True
        ).astype(jnp.float32),
        lax.psum_scatter(
            grad_total[1].astype(jnp.bfloat16), "pair", scatter_dimension=0, tiled=True
        ).astype(jnp.float32),
        lax.psum_scatter(
            grad_total[2].astype(jnp.bfloat16), "pair", scatter_dimension=0, tiled=True
        ).astype(jnp.float32),
        lax.psum_scatter(
            grad_total[3].astype(jnp.bfloat16), "pair", scatter_dimension=0, tiled=True
        ).astype(jnp.float32),
        lax.psum_scatter(
            grad_total[4].astype(jnp.bfloat16), "pair", scatter_dimension=1, tiled=True
        ).astype(jnp.float32),
        lax.psum_scatter(
            grad_total[5].astype(jnp.bfloat16), "pair", scatter_dimension=0, tiled=True
        ).astype(jnp.float32),
        lax.psum_scatter(
            grad_total[6].astype(jnp.bfloat16), "pair", scatter_dimension=1, tiled=True
        ).astype(jnp.float32),
        lax.psum_scatter(
            grad_total[7].astype(jnp.bfloat16), "pair", scatter_dimension=1, tiled=True
        ).astype(jnp.float32),
        lax.psum_scatter(
            grad_total[8].astype(jnp.bfloat16), "pair", scatter_dimension=1, tiled=True
        ).astype(jnp.float32),
    )
    summed = lax.psum(
        (
            shares[0],
            shares[1],
            shares[2],
            shares[3],
            shares[4],
            shares[5],
            shares[6],
            shares[7],
            shares[8],
        ),
        "dp",
    )
    return (section_out[None], input_grad[None]) + tuple((leaf[None] for leaf in summed))


def solution(mesh):
    return jax.shard_map(
        local,
        mesh=mesh,
        in_specs=(
            P(("dp", "pair"), None),
            P(("dp", "pair"), None),
            P(("dp", "pair"), None),
            P(("dp", "pair")),
            P(("dp", "pair"), None),
            P("pipe", "pair", None),
            P("pipe", "pair", None),
            P("pipe", "pair", None),
            P("pipe", "pair", None),
            P("pipe", None, "pair"),
            P("pipe", "pair"),
            P("pipe", None, "pair"),
            P("pipe", None, "pair"),
            P("pipe", None, "pair"),
        ),
        out_specs=(
            P("pipe", ("dp", "pair"), None),
            P("pipe", ("dp", "pair"), None),
            P("pipe", "pair", None),
            P("pipe", "pair", None),
            P("pipe", "pair", None),
            P("pipe", "pair", None),
            P("pipe", None, "pair"),
            P("pipe", "pair"),
            P("pipe", None, "pair"),
            P("pipe", None, "pair"),
            P("pipe", None, "pair"),
        ),
        check_vma=False,
    )
```

profile of v0, /device:TPU:0, one launch (start us, length us, event | category | flops | bytes accessed | tf_op | source)
XLA Modules:
  0.0 842.0 jit_solution(16606748714593569604)
XLA Ops:
  10.1 1.9 all-gather.5
  21.8 3.2 all-gather.14.cloned.1.call-done
  25.0 3.0 fusion.43
  32.1 4.9 all-gather.16.cloned.1.call-done
  39.9 14.2 %all-gather.18.cloned.1.call-done = bf16[1,768,3072]{2,1,0:T(8,128)(2,1)} async-done(((bf16[1,384,3072]{2,1,0:T(8,128)(2,1)}), bf16[1,768,3072]{2,1,0:T(8,128)(2,1)}) %all-gather.18.cloned.1.call-update) | async-done | bytes 4718608 | tf_op jit(solution)/shard_map/all_gather | solution.py:230
  54.2 4.0 fusion.24
  58.1 13.1 %all-gather.20.cloned.1.call-done = bf16[1,3072,768]{2,1,0:T(8,128)(2,1)} async-done(((bf16[1,1536,768]{2,1,0:T(8,128)(2,1)}), bf16[1,3072,768]{2,1,0:T(8,128)(2,1)}) %all-gather.20.cloned.1.call-update) | async-done | bytes 4718608 | tf_op jit(solution)/shard_map/all_gather | solution.py:231
  71.3 4.5 fusion.332
  77.5 4.9 collective-permute-start
  104.2 4.1 fusion.27
  108.5 1.9 fusion.333
  112.3 5.4 collective-permute-start.1
  132.1 2.7 fusion.140
  138.8 2.5 fusion.334
  146.8 3.8 fusion.51
  150.7 2.3 multiply_reduce_fusion.5
  178.3 1.9 copy.130
  184.0 4.4 fusion.194
  203.5 3.4 fusion.336
  207.0 2.2 fusion.337
  214.7 5.5 fusion.58
  220.3 2.4 multiply_reduce_fusion.4
  226.4 2.7 fusion.146
  238.4 3.4 fusion.191
  244.5 8.5 %collective-permute-done.3 = bf16[240,768]{1,0:T(8,128)(2,1)S(1)} collective-permute-done((bf16[240,768]{1,0:T(8,128)(2,1)S(1)}, bf16[240,768]{1,0:T(8,128)(2,1)S(1)}, u32[]{:S(2)}, u32[]{:S(2)}) %collective-permute-start.3) | collective-permute-done | bytes 368672 | tf_op jit(solution)/shard_map/ppermute | solution.py:23
  253.8 6.8 fusion.65
  271.1 3.1 bitcast_convert_fusion.5
  274.4 1.9 multiply_reduce_fusion
  279.8 2.0 fusion.199
  284.4 4.0 bitcast_convert_fusion.2
  295.4 4.7 bitcast_convert_fusion.1
  304.1 3.2 fusion.308
  309.7 5.2 bitcast_convert_fusion
  319.5 2.2 bitcast_convert_fusion.7
  321.7 3.5 bitcast_convert_fusion.6
  325.2 4.4 bitcast_convert_fusion.4
  329.6 4.1 reduce-scatter.23.cloned.1.call-done
  333.7 4.2 bitcast_convert_fusion.3
  343.6 2.5 all-reduce.2
  346.1 2.6 fusion.200
  351.8 3.7 reduce-scatter.27.cloned.1.call-done
  356.5 10.0 %reduce-scatter.29.cloned.1.call-done = bf16[384,2]{1,0:T(8,128)(2,1)} async-done(((bf16[768,2]{1,0:T(8,128)(2,1)}), bf16[384,2]{1,0:T(8,128)(2,1)}) %reduce-scatter.29.cloned.1.call-update) | async-done | bytes 1552
  367.5 9.9 %reduce-scatter.31.cloned.1.call-done = bf16[384,2]{1,0:T(8,128)(2,1)} async-done(((bf16[768,2]{1,0:T(8,128)(2,1)}), bf16[384,2]{1,0:T(8,128)(2,1)}) %reduce-scatter.31.cloned.1.call-update) | async-done | bytes 1552
  378.4 39.3 %all-reduce.3 = (f32[1,2,384]{2,1,0:T(2,128)}, f32[1,1536]{1,0:T(1,128)}, f32[1,2,384]{2,1,0:T(2,128)}, f32[1,2,384]{2,1,0:T(2,128)}, f32[1,2,384]{2,1,0:T(2,128)}) all-reduce(f32[1,2,384]{2,1,0:T(2,128)S(1)} %bitcast_convert_fusion.11, f32[1,1536]{1,0:T(1,128)S(1)} %broadcast_in_dim.210, ...), channel_id=1, replica_groups=mesh['dp'=8,'pipe'=2,'pair'=2] {'dp'}, use_global_device_ids=true, to_apply=%region_55.56 | all-reduce | flops 4608 | bytes 36864 | tf_op jit(solution)/shard_map/psum | solution.py:340
  417.7 406.7 %all-reduce.7.cloned.1.call-done = (f32[1,384,2304]{2,1,0:T(8,128)}, f32[1,384,768]{2,1,0:T(8,128)}, f32[1,384,3072]{2,1,0:T(8,128)}, f32[1,1536,768]{2,1,0:T(8,128)}) async-done(((f32[1,384,2304]{2,1,0:T(8,128)}, f32[1,384,768]{2,1,0:T(8,128)}, f32[1,384,3072]{2,1,0:T(8,128)}, f32[1,1536,768]{2,1,0:T(8,128)}), (f32[1,384,2304]{2,1,0:T(8,128)}, f32[1,384,768]{2,1,0:T(8,128)}, f32[1,384,3072]{2,1,0:T(8,128)}, ...) | async-done | bytes 14155792 | tf_op jit(solution)/shard_map/psum | solution.py:340
  824.4 4.2 copy.178
  829.6 2.4 copy.180
  833.0 2.2 copy.181
  (683 shorter events, 180.6 us)
Async XLA Ops:
  7.2 17.8 %all-gather.14.cloned.1.call-start = ((), (), s32[]{:S(2)}) async-start(), calls=%async_computation.12 | async-start | bytes 5308416 | tf_op jit(solution)/shard_map/all_gather | solution.py:228
  7.9 7.7 copy-start.184
  8.0 9.5 %copy-start.180 = (s32[2,176]{1,0:T(2,128)S(1)}, s32[2,176]{1,0:T(2,128)}, u32[]{:S(2)}) copy-start(s32[2,176]{1,0:T(2,128)} %param.16) | copy-start | bytes 4228
  8.0 9.5 %copy-start.152 = (bf16[1,1536]{1,0:T(2,128)(2,1)S(1)}, bf16[1,1536]{1,0:T(2,128)(2,1)}, u32[]{:S(2)}) copy-start(bf16[1,1536]{1,0:T(2,128)(2,1)} %param.24) | copy-start | bytes 9220
  8.0 11.3 %copy-start.186 = (s32[2]{0:T(128)S(1)}, s32[2]{0:T(128)}, u32[]{:S(2)}) copy-start(s32[2]{0:T(128)} %param.17) | copy-start | bytes 28
  8.0 12.8 %copy-start.179 = (s32[2,176]{1,0:T(2,128)S(1)}, s32[2,176]{1,0:T(2,128)}, u32[]{:S(2)}) copy-start(s32[2,176]{1,0:T(2,128)} %param.18) | copy-start | bytes 4228
  8.0 17.0 %copy-start.74 = (bf16[480,768]{1,0:T(8,128)(2,1)S(1)}, bf16[480,768]{1,0:T(8,128)(2,1)}, u32[]{:S(2)}) copy-start(bf16[480,768]{1,0:T(8,128)(2,1)} %param.14) | copy-start | bytes 2211844
  8.0 29.0 %all-gather.16.cloned.1.call-start = ((), (), s32[]{:S(2)}) async-start(), calls=%async_computation.13 | async-start | bytes 1769472 | tf_op jit(solution)/shard_map/all_gather | solution.py:229
  8.8 45.4 %all-gather.18.cloned.1.call-start = ((), (), s32[]{:S(2)}) async-start(), calls=%async_computation.14 | async-start | bytes 7077888 | tf_op jit(solution)/shard_map/all_gather | solution.py:230
  9.5 61.7 %all-gather.20.cloned.1.call-start = ((), (), s32[]{:S(2)}) async-start(), calls=%async_computation.15 | async-start | bytes 7077888 | tf_op jit(solution)/shard_map/all_gather | solution.py:231
  10.1 309.4 %reduce-scatter.19.cloned.1.call-start = ((), (), s32[]{:S(2)}) async-start(), calls=%async_computation.9 | async-start | bytes 1769472 | tf_op jit(solution)/shard_map/reduce_scatter | solution.py:315
  13.8 14.2 %copy-start.126 = (bf16[1,2,768]{2,1,0:T(2,128)(2,1)}, bf16[1,2,768]{2,1,0:T(2,128)(2,1)S(1)}, u32[]{:S(2)}) copy-start(bf16[1,2,768]{2,1,0:T(2,128)(2,1)S(1)} %all-gather.4) | copy-start | bytes 9220
  19.3 34.9 %copy-start.139 = (f32[1,3072]{1,0:T(1,128)}, f32[1,3072]{1,0:T(1,128)S(1)}, u32[]{:S(2)}) copy-start(f32[1,3072]{1,0:T(1,128)S(1)} %convert_element_type.519) | copy-start | bytes 36868
  20.1 51.1 %copy-start.133 = (f32[768]{0:T(1024)}, f32[768]{0:T(1024)S(1)}, u32[]{:S(2)}) copy-start(f32[768]{0:T(1024)S(1)} %get-tuple-element.44) | copy-start | bytes 9220
  20.7 50.5 %copy-start.136 = (f32[768]{0:T(1024)}, f32[768]{0:T(1024)S(1)}, u32[]{:S(2)}) copy-start(f32[768]{0:T(1024)S(1)} %get-tuple-element.42) | copy-start | bytes 9220
  20.7 16.3 %copy-start.127 = (f32[768]{0:T(1024)}, f32[768]{0:T(1024)S(1)}, u32[]{:S(2)}) copy-start(f32[768]{0:T(1024)S(1)} %get-tuple-element.46) | copy-start | bytes 9220
  20.7 50.5 %copy-start.167 = (f32[768]{0:T(1024)}, f32[768]{0:T(1024)S(1)}, u32[]{:S(2)}) copy-start(f32[768]{0:T(1024)S(1)} %get-tuple-element.45) | copy-start | bytes 9220
  20.8 7.4 copy-start.118
  20.8 7.4 copy-start.121
  21.8 9.6 %copy-start.65 = (pred[240,240]{0,1:T(8,128)(4,1)}, pred[240,240]{0,1:T(8,128)(4,1)S(1)}, u32[]{:S(2)}) copy-start(pred[240,240]{0,1:T(8,128)(4,1)S(1)} %get-tuple-element.119) | copy-start | bytes 172804
  31.3 7.5 copy-start.109
  32.1 22.1 %copy-start.80 = (bf16[12,64,240]{2,1,0:T(8,128)(2,1)}, bf16[12,64,240]{2,1,0:T(8,128)(2,1)S(1)}, u32[]{:S(2)}) copy-start(bf16[12,64,240]{2,1,0:T(8,128)(2,1)S(1)} %fusion.142) | copy-start | bytes 1105924
  38.9 32.4 %copy-start.142 = (f32[240]{0:T(256)}, f32[240]{0:T(256)S(1)}, u32[]{:S(2)}) copy-start(f32[240]{0:T(256)S(1)} %broadcast_multiply_fusion.11) | copy-start | bytes 2884
  39.9 31.3 %copy-start.157 = (f32[240]{0:T(256)}, f32[240]{0:T(256)S(1)}, u32[]{:S(2)}) copy-start(f32[240]{0:T(256)S(1)} %add_rsqrt_fusion.5) | copy-start | bytes 2884
  58.1 13.1 %copy-start.12 = (f32[240,3072]{1,0:T(8,128)}, f32[240,3072]{1,0:T(8,128)S(1)}, u32[]{:S(2)}) copy-start(f32[240,3072]{1,0:T(8,128)S(1)} %fusion.24) | copy-start | bytes 8847364
  75.7 15.1 %copy-start.2 = (bf16[1,768,2304]{2,1,0:T(8,128)(2,1)S(1)}, bf16[1,768,2304]{2,1,0:T(8,128)(2,1)}, u32[]{:S(2)}) copy-start(bf16[1,768,2304]{2,1,0:T(8,128)(2,1)} %all-gather.14.cloned.1.call-done) | copy-start | bytes 10616836
  77.5 12.2 %collective-permute-start = (bf16[240,768]{1,0:T(8,128)(2,1)}, bf16[240,768]{1,0:T(8,128)(2,1)}, u32[]{:S(2)}, u32[]{:S(2)}) collective-permute-start(bf16[240,768]{1,0:T(8,128)(2,1)} %add_convert_fusion.2), channel_id=1, source_target_pairs={{0,2},{1,3},{4,6},{5,7},{8,10},{9,11},{12,14},{13,15},{16,18},{17,... | collective-permute-start | bytes 1105928 | tf_op jit(solution)/shard_map/ppermute | solution.py:23
  112.3 12.3 %collective-permute-start.1 = (bf16[240,768]{1,0:T(8,128)(2,1)}, bf16[240,768]{1,0:T(8,128)(2,1)}, u32[]{:S(2)}, u32[]{:S(2)}) collective-permute-start(bf16[240,768]{1,0:T(8,128)(2,1)} %add_convert_fusion.1), channel_id=1, source_target_pairs={{0,2},{1,3},{4,6},{5,7},{8,10},{9,11},{12,14},{13,15},{16,18},{17,... | collective-permute-start | bytes 1105928 | tf_op jit(solution)/shard_map/ppermute | solution.py:23
  136.4 16.6 %copy-start.8 = (f32[3,240,768]{2,1,0:T(8,128)}, f32[3,240,768]{2,1,0:T(8,128)S(1)}, u32[]{:S(2)}) copy-start(f32[3,240,768]{2,1,0:T(8,128)S(1)} %pad_maximum_fusion.3) | copy-start | bytes 6635524
  143.7 7.0 copy-start.153
  152.9 25.3 %copy-start.174 = (f32[240]{0:T(256)}, f32[240]{0:T(256)S(1)}, u32[]{:S(2)}) copy-start(f32[240]{0:T(256)S(1)} %get-tuple-element.25) | copy-start | bytes 2884
  178.2 41.9 %copy-start.155 = (f32[240]{0:T(256)}, f32[240]{0:T(256)S(1)}, u32[]{:S(2)}) copy-start(f32[240]{0:T(256)S(1)} %broadcast_multiply_fusion) | copy-start | bytes 2884
  188.4 24.2 %collective-permute-start.2 = (bf16[240,768]{1,0:T(8,128)(2,1)}, bf16[240,768]{1,0:T(8,128)(2,1)}, u32[]{:S(2)}, u32[]{:S(2)}) collective-permute-start(bf16[240,768]{1,0:T(8,128)(2,1)} %fusion.194), channel_id=1, source_target_pairs={{2,0},{3,1},{6,4},{7,5},{10,8},{11,9},{14,12},{15,13},{18,16},{19,... | collective-permute-start | bytes 1105928 | tf_op jit(solution)/shard_map/ppermute | solution.py:23
  206.9 7.7 slice-start.14
  212.6 7.6 slice-start.6
  238.4 14.6 %copy-start.79 = (bf16[480,768]{1,0:T(8,128)(2,1)S(1)}, bf16[480,768]{1,0:T(8,128)(2,1)}, u32[]{:S(2)}) copy-start(bf16[480,768]{1,0:T(8,128)(2,1)} %param.15) | copy-start | bytes 2211844
  241.8 11.9 %copy-start.102 = (bf16[240,768]{1,0:T(8,128)(2,1)}, bf16[240,768]{1,0:T(8,128)(2,1)S(1)}, u32[]{:S(2)}) copy-start(bf16[240,768]{1,0:T(8,128)(2,1)S(1)} %fusion.191) | copy-start | bytes 1105924
  241.9 11.1 %collective-permute-start.3 = (bf16[240,768]{1,0:T(8,128)(2,1)S(1)}, bf16[240,768]{1,0:T(8,128)(2,1)S(1)}, u32[]{:S(2)}, u32[]{:S(2)}) collective-permute-start(bf16[240,768]{1,0:T(8,128)(2,1)S(1)} %fusion.191), channel_id=1, source_target_pairs={{2,0},{3,1},{6,4},{7,5},{10,8},{11,9},{14,12},{15,13},{18,16},{19,... | collective-permute-start | bytes 1105928 | tf_op jit(solution)/shard_map/ppermute | solution.py:23
  243.3 17.3 %slice-start.8 = ((s8[4718592]{0:T(1024)(128)(4,1)}), s8[4194304]{0:T(1024)(128)(4,1)S(1)}, s32[]{:S(2)}) async-start(s8[4718592]{0:T(1024)(128)(4,1)} %bitcast.582), calls=%async_computation.29 | async-start | bytes 8388608
  253.8 6.8 copy-start.72
  274.2 47.5 %reduce-scatter.17.cloned.1.call-start = ((), (), s32[]{:S(2)}) async-start(), calls=%async_computation.8 | async-start | bytes 5308416 | tf_op jit(solution)/shard_map/reduce_scatter | solution.py:312
  288.6 36.6 %reduce-scatter.21.cloned.1.call-start = ((), (), s32[]{:S(2)}) async-start(), calls=%async_computation.10 | async-start | bytes 7077888 | tf_op jit(solution)/shard_map/reduce_scatter | solution.py:318
  300.2 33.5 %reduce-scatter.23.cloned.1.call-start = ((), (), s32[]{:S(2)}) async-start(), calls=%async_computation.11 | async-start | bytes 7077888 | tf_op jit(solution)/shard_map/reduce_scatter | solution.py:321
  314.9 36.0 %reduce-scatter.25.cloned.1.call-start = ((), (), s32[]{:S(2)}) async-start(), calls=%async_computation.16 | async-start | bytes 294912
  316.6 38.9 %reduce-scatter.27.cloned.1.call-start = ((), (), s32[]{:S(2)}) async-start(), calls=%async_computation.17 | async-start | bytes 294912
  317.5 49.0 %reduce-scatter.29.cloned.1.call-start = ((), (), s32[]{:S(2)}) async-start(), calls=%async_computation.18 | async-start | bytes 294912
  318.5 58.9 %reduce-scatter.31.cloned.1.call-start = ((), (), s32[]{:S(2)}) async-start(), calls=%async_computation.19 | async-start | bytes 294912
  319.4 504.9 %all-reduce.7.cloned.1.call-start = ((), (), s32[]{:S(2)}) async-start(), calls=%async_computation.20 | async-start | bytes 28311552 | tf_op jit(solution)/shard_map/psum | solution.py:340
  (173 other events, 472.3 us)
Sparse Core Ops, SparseCore 0:
  9.6 15.3 all-gather.13
  26.5 10.3 all-gather.15
  38.5 15.5 all-gather.17
  55.6 15.6 all-gather.19
  274.3 8.6 reduce-scatter.18
  288.7 11.4 reduce-scatter.16
  303.1 13.7 reduce-scatter.20
  319.9 13.7 reduce-scatter.22
  335.9 8.7 reduce-scatter.24
  346.7 8.7 reduce-scatter.26
  357.7 8.7 reduce-scatter.28
  368.6 8.7 reduce-scatter.30
  382.6 441.6 all-reduce.6
where the time goes:
time: 851 us; the launch traced here: 842 us
  waiting for transfers between devices  484 us (57%)
  matrix products  112 us (13%)
  local copies, waits for them, and re-layouts  99.1 us (12%)
  other arithmetic  64.4 us (8%)
  blocking collectives  50.8 us (6%)
  between operations  17.9 us (2%)
  starting transfers between devices  14.4 us (2%)
    psum x1, waiting for transfers between devices, local(): lax.psum((shares[0], shares[1], shares[2], shares[3], shares[4], shares[5...  407 us
    unnamed x421, local copies, waits for them, and re-layouts  40.3 us
    psum x1, blocking collectives, local(): lax.psum((shares[0], shares[1], shares[2], shares[3], shares[4], shares[5...  39.3 us
    unnamed x17, waiting for transfers between devices  26.4 us
    dynamic_slice x14, local copies, waits for them, and re-layouts, local(): lax.dynamic_index_in_dim(leaf, batch_index + section_index, 0, keepdims=F...  21.6 us
  transfers between devices with their start and end apart: 17, of which 12 were waited for; matrix products, arithmetic and copies ran while one was open for 13% of the time, Pallas kernels for 0%

commit v1 on v0

--- a/solution.py
+++ b/solution.py
@@ -207,6 +207,103 @@
     return (grad_wqkv, grad_wout, grad_up, grad_down, grad_bias_qv, grad_bias_up, grad_bias_res)
 
 
+def ring_levels(total):
+    sizes = []
+    while total > 1:
+        size = max([k for k in range(2, 9) if total % k == 0], default=total)
+        sizes.append(size)
+        total //= size
+    return sizes
+
+
+def ring_route(total, stride, size):
+    order = list(range(size))
+    if total == size and size % 2 == 0:
+        order = list(range(0, size, 2)) + list(range(size - 1, 0, -2))
+    place = [0] * total
+    route = []
+    for device in range(total):
+        place[device] = order.index(device // stride % size)
+    for device in range(total):
+        after = order[(place[device] + 1) % size]
+        base = device - device // stride % size * stride
+        target = base + after * stride
+        route.append((device * 2, target * 2))
+        route.append((target * 2 + 1, device * 2 + 1))
+    return (place, route)
+
+
+def ring_place(total, stride, size):
+    place, route = ring_route(total, stride, size)
+    at = jnp.asarray(place, jnp.int32)[lax.axis_index("dp")]
+    at = jnp.where(lax.axis_index("pair") == 0, at, (size - at) % size)
+    return (at, route)
+
+
+def ring_scatter(terms, total, stride, size):
+    at, route = ring_place(total, stride, size)
+    parts = range(len(terms))
+
+    def term(part, step):
+        index = (at + step + 2 * size) % size
+        value = 0.0
+        for leaf in terms[part]:
+            rows = leaf.shape[0] // size
+            piece = lax.dynamic_slice_in_dim(leaf, index * rows, rows, 0)
+            value = value + piece.astype(jnp.float32)
+        return value
+
+    running = [term(part, 0).astype(jnp.bfloat16) for part in parts]
+    for step in range(size - 1):
+        for part in parts:
+            arrived = lax.ppermute(running[part], ("dp", "pair"), route)
+            running[part] = (arrived.astype(jnp.float32) + term(part, -step - 1)).astype(
+                jnp.bfloat16
+            )
+    return running
+
+
+def ring_gather(pieces, total, stride, size, dtype):
+    at, route = ring_place(total, stride, size)
+    running = list(pieces)
+    totals = [
+        jnp.zeros((size * leaf.shape[0],) + leaf.shape[1:], dtype) for leaf in pieces
+    ]
+    for step in range(size):
+        index = (at + 1 - step + 2 * size) % size
+        for part, leaf in enumerate(running):
+            totals[part] = lax.dynamic_update_slice_in_dim(
+                totals[part], leaf.astype(dtype), index * leaf.shape[0], 0
+            )
+        if step < size - 1:
+            running = [lax.ppermute(leaf, ("dp", "pair"), route) for leaf in running]
+    return totals
+
+
+def ring_sum(terms):
+    total = lax.axis_size("dp")
+    levels = []
+    stride = 1
+    for size in ring_levels(total):
+        levels.append((stride, size))
+        stride *= size
+    for stride, size in levels:
+        pieces = ring_scatter(terms, total, stride, size)
+        terms = [(piece,) for piece in pieces]
+    for depth, (stride, size) in enumerate(levels[::-1]):
+        dtype = jnp.float32 if depth == len(levels) - 1 else jnp.bfloat16
+        pieces = ring_gather(pieces, total, stride, size, dtype)
+    return pieces
+
+
+def pair_halves(total, axis):
+    half = total.shape[axis] // 2
+    me = lax.axis_index("pair")
+    own = lax.dynamic_slice_in_dim(total, me * half, half, axis)
+    away = lax.dynamic_slice_in_dim(total, (1 - me) * half, half, axis)
+    return (own, lax.ppermute(away.astype(jnp.bfloat16), "pair", [(0, 1), (1, 0)]))
+
+
 def local(
     inputs,
     cotangent,
@@ -251,12 +348,10 @@
         output_list.append(layer_out)
         if moment < MB:
             received = passed_along(layer_out, "pipe", 1)
-    kept_stack = jax.tree.map(lambda *leaves: jnp.stack(leaves), *kept_list)
-    output_stack = jnp.stack(output_list)
     section_out = jnp.concatenate(
         [
-            lax.dynamic_index_in_dim(output_stack, batch_number + section_index, 0, keepdims=False)
-            for batch_number in range(MB)
+            jnp.where(section_index == 0, output_list[number], output_list[number + 1])
+            for number in range(MB)
         ],
         axis=0,
     )
@@ -273,12 +368,7 @@
         )
         grad_now = jnp.where(section_index == 1, own_grad, received)
         grad_now = jnp.where(valid, grad_now, jnp.zeros_like(grad_now))
-        saved = jax.tree.map(
-            lambda leaf: lax.dynamic_index_in_dim(
-                leaf, batch_index + section_index, 0, keepdims=False
-            ),
-            kept_stack,
-        )
+        saved = kept_list[MB - moment]
         keep_now = lax.dynamic_slice_in_dim(keep_all, batch_index * DOC_MB, DOC_MB, 0)
         grad_in, norm_terms, factors = layer_backward(grad_now, saved, keep_now, layer_weights)
         if norm_total is None:
@@ -289,69 +379,39 @@
         factor_list.append(factors)
         if moment < MB:
             received = passed_along(grad_in, "pipe", -1)
-    grad_stack = jnp.stack(grad_list)
     input_grad = jnp.concatenate(
         [
-            lax.dynamic_index_in_dim(
-                grad_stack, MB - batch_number - section_index, 0, keepdims=False
-            )
-            for batch_number in range(MB)
+            jnp.where(section_index == 0, grad_list[MB - number], grad_list[MB - number - 1])
+            for number in range(MB)
         ],
         axis=0,
     )
-    factor_stack = jax.tree.map(lambda *leaves: jnp.stack(leaves), *factor_list)
-    first_valid = 1 - section_index
     chosen = jax.tree.map(
-        lambda leaf: lax.dynamic_slice_in_dim(leaf, first_valid, MB, 0).reshape(
-            (MB * row_count,) + leaf.shape[2:]
+        lambda *leaves: jnp.concatenate(
+            [
+                jnp.where(section_index == 0, leaves[number + 1], leaves[number])
+                for number in range(MB)
+            ],
+            axis=0,
         ),
-        factor_stack,
+        *factor_list,
     )
     grad_total = weight_products(chosen) + (norm_total[0], norm_total[1])
-    shares = (
-        lax.psum_scatter(
-            grad_total[0].astype(jnp.bfloat16), "pair", scatter_dimension=0, tiled=True
-        ).astype(jnp.float32),
-        lax.psum_scatter(
-            grad_total[1].astype(jnp.bfloat16), "pair", scatter_dimension=0, tiled=True
-        ).astype(jnp.float32),
-        lax.psum_scatter(
-            grad_total[2].astype(jnp.bfloat16), "pair", scatter_dimension=0, tiled=True
-        ).astype(jnp.float32),
-        lax.psum_scatter(
-            grad_total[3].astype(jnp.bfloat16), "pair", scatter_dimension=0, tiled=True
-        ).astype(jnp.float32),
-        lax.psum_scatter(
-            grad_total[4].astype(jnp.bfloat16), "pair", scatter_dimension=1, tiled=True
-        ).astype(jnp.float32),
-        lax.psum_scatter(
-            grad_total[5].astype(jnp.bfloat16), "pair", scatter_dimension=0, tiled=True
-        ).astype(jnp.float32),
-        lax.psum_scatter(
-            grad_total[6].astype(jnp.bfloat16), "pair", scatter_dimension=1, tiled=True
-        ).astype(jnp.float32),
-        lax.psum_scatter(
-            grad_total[7].astype(jnp.bfloat16), "pair", scatter_dimension=1, tiled=True
-        ).astype(jnp.float32),
-        lax.psum_scatter(
-            grad_total[8].astype(jnp.bfloat16), "pair", scatter_dimension=1, tiled=True
-        ).astype(jnp.float32),
-    )
-    summed = lax.psum(
-        (
-            shares[0],
-            shares[1],
-            shares[2],
-            shares[3],
-            shares[4],
-            shares[5],
-            shares[6],
-            shares[7],
-            shares[8],
-        ),
-        "dp",
-    )
-    return (section_out[None], input_grad[None]) + tuple((leaf[None] for leaf in summed))
+    halves = [pair_halves(leaf, 0) for leaf in grad_total[:4]]
+    order = (3, 2, 0, 1)
+    summed_big = ring_sum([halves[k] for k in order])
+    big = [None] * 4
+    for slot, k in enumerate(order):
+        big[k] = summed_big[slot]
+    small_axes = (1, 0, 1, 1, 1)
+    shares = [
+        lax.psum_scatter(leaf, "pair", scatter_dimension=axis, tiled=True)
+        for leaf, axis in zip(grad_total[4:], small_axes)
+    ]
+    small = lax.psum(tuple(shares), "dp")
+    return (section_out[None], input_grad[None]) + tuple(
+        (leaf[None] for leaf in tuple(big) + tuple(small))
+    )
 
 
 def solution(mesh):

time: 851 us -> 542 us (0.64)
  waiting for transfers between devices: 484 us -> 183 us
  local copies, waits for them, and re-layouts: 99.1 us -> 65.6 us
  starting transfers between devices: 14.4 us -> 46 us
  matrix products: 112 us -> 97 us
    psum x1 -> x0, waiting for transfers between devices: 407 us -> none  [local(): lax.psum((shares[0], shares[1], shares[2], shares[3], shares[4], shares[5...]
    ppermute x0 -> x60, waiting for transfers between devices: none -> 130 us  [the longest x28 77.1 us: ring_gather(): running = [lax.ppermute(leaf, ('dp', 'pair'), route) for leaf in running]]
    ppermute x0 -> x60, starting transfers between devices: none -> 33.2 us  [the longest x28 18.8 us: ring_scatter(): arrived = lax.ppermute(running[part], ('dp', 'pair'), route)]
    convert_element_type x3 -> x28, other arithmetic: 0.13 us -> 31.6 us  [the longest x24 27.9 us: ring_scatter(): (arrived.astype(jnp.float32) + term(part, -step - 1)).astype(jnp.bfloat16)]
    another operation x28 -> x0, other arithmetic: 23.8 us -> none  [the longest x15 13.7 us: local(): kept_stack = jax.tree.map(lambda *leaves: jnp.stack(leaves), *kept_list)]
    unnamed x17 -> x12, waiting for transfers between devices: 26.4 us -> 3.68 us
    dynamic_slice x14 -> x1, local copies, waits for them, and re-layouts: 21.6 us -> 1.24 us  [ring_place(): at = jnp.asarray(place, jnp.int32)[lax.axis_index('dp')]]
    broadcast_in_dim x8 -> x0, other arithmetic: 14.3 us -> none  [local(): leaf[None]]
  transfers between devices with their start and end apart: 17 -> 72, of which waited for: 12 -> 54; matrix products, arithmetic and copies ran while one was open for 13% -> 19% of each run, Pallas kernels for 0% -> 0%
where the time goes in v1:
time: 542 us; the launch traced here: 533 us
  waiting for transfers between devices  183 us (34%)
  matrix products  97 us (18%)
  other arithmetic  71.6 us (13%)
  local copies, waits for them, and re-layouts  65.6 us (12%)
  blocking collectives  50.3 us (9%)
  starting transfers between devices  46 us (8%)
  between operations  19.9 us (4%)
    ppermute x28, waiting for transfers between devices, ring_gather(): running = [lax.ppermute(leaf, ('dp', 'pair'), route) for leaf in running]  77.1 us
    ppermute x28, waiting for transfers between devices, ring_scatter(): arrived = lax.ppermute(running[part], ('dp', 'pair'), route)  52.6 us
    psum x1, blocking collectives, local(): small = lax.psum(tuple(shares), 'dp')  37.9 us
    unnamed x454, local copies, waits for them, and re-layouts  32.4 us
    convert_element_type x24, other arithmetic, ring_scatter(): (arrived.astype(jnp.float32) + term(part, -step - 1)).astype(jnp.bfloat16)  27.9 us
    ppermute x4, waiting for transfers between devices, passed_along(): return lax.ppermute(block, axis, route)  20.3 us
    ppermute x28, starting transfers between devices, ring_scatter(): arrived = lax.ppermute(running[part], ('dp', 'pair'), route)  18.8 us
    dot_general x3, matrix products, layer_backward(): jnp.einsum('rd,fd->rf', branch_low, w_down, preferred_element_type=jnp.fl...  14.9 us
  transfers between devices with their start and end apart: 72, of which 54 were waited for; matrix products, arithmetic and copies ran while one was open for 19% of the time, Pallas kernels for 0%

profile of v1, /device:TPU:0, one launch (start us, length us, event | category | flops | bytes accessed | tf_op | source)
XLA Modules:
  0.0 533.5 jit_solution(8201389550094393735)
XLA Ops:
  22.3 2.7 all-gather.14.cloned.1.call-done
  25.0 3.0 fusion.43
  40.1 14.0 %all-gather.18.cloned.1.call-done = bf16[1,768,3072]{2,1,0:T(8,128)(2,1)} async-done(((bf16[1,384,3072]{2,1,0:T(8,128)(2,1)}), bf16[1,768,3072]{2,1,0:T(8,128)(2,1)}) %all-gather.18.cloned.1.call-update) | async-done | bytes 4718608 | tf_op jit(solution)/shard_map/all_gather | solution.py:327
  54.2 5.6 %fusion.24 = f32[240,3072]{1,0:T(8,128)} fusion(bf16[1,768,3072]{2,1,0:T(8,128)(2,1)} %all-gather.18.cloned.1.call-done, f32[3072]{0:T(1024)S(1)} %bitcast.410, f32[240,768]{1,0:T(8,128)} %copy-done.23, f32[768]{0:T(1024)S(1)} %copy-done.127, f32[768]{0:T(1024)S(1)} %copy-done.130, f32[240]{0:T(256)S(1)} %fusion.193, f32[240]{0:T(256)S(1)} %broadcast_multiply_fusion.5), kind=kOutput, calls=%fused_computation.34 | convolution fusion | flops 1134120960 | bytes 8425344 | tf_op jit(solution)/shard_map/dot_general | solution.py:83
  59.7 11.5 %all-gather.20.cloned.1.call-done = bf16[1,3072,768]{2,1,0:T(8,128)(2,1)} async-done(((bf16[1,1536,768]{2,1,0:T(8,128)(2,1)}), bf16[1,3072,768]{2,1,0:T(8,128)(2,1)}) %all-gather.20.cloned.1.call-update) | async-done | bytes 4718608 | tf_op jit(solution)/shard_map/all_gather | solution.py:328
  71.2 5.4 %fusion.225 = (f32[240]{0:T(256)S(1)}, f32[240,768]{1,0:T(8,128)S(1)}) fusion(f32[768]{0:T(1024)S(1)} %copy-done.180, bf16[1,3072,768]{2,1,0:T(8,128)(2,1)} %all-gather.20.cloned.1.call-done, f32[240,3072]{1,0:T(8,128)} %fusion.24, f32[768]{0:T(1024)S(1)} %copy-done.127, f32[768]{0:T(1024)S(1)} %copy-done.130, f32[240]{0:T(256)S(1)} %fusion.193, ...), kind=kOutput, calls=%fused_computation.419 | convolution fusion | flops 1140387584 | bytes 9154368 | tf_op jit(solution)/shard_map/dot_general | solution.py:86
  77.6 4.0 collective-permute-start
  81.6 8.1 %collective-permute-done = bf16[240,768]{1,0:T(8,128)(2,1)S(1)} collective-permute-done((bf16[240,768]{1,0:T(8,128)(2,1)S(1)}, bf16[240,768]{1,0:T(8,128)(2,1)S(1)}, u32[]{:S(2)}, u32[]{:S(2)}) %collective-permute-start) | collective-permute-done | bytes 368672 | tf_op jit(solution)/shard_map/ppermute | solution.py:23
  111.1 5.4 %collective-permute-start.1 = (bf16[240,768]{1,0:T(8,128)(2,1)}, bf16[240,768]{1,0:T(8,128)(2,1)}, u32[]{:S(2)}, u32[]{:S(2)}) collective-permute-start(bf16[240,768]{1,0:T(8,128)(2,1)} %get-tuple-element.77), channel_id=1, source_target_pairs={{0,2},{1,3},{4,6},{5,7},{8,10},{9,11},{12,14},{13,15},{16,18},{17,... | collective-permute-start | bytes 1105928 | tf_op jit(solution)/shard_map/ppermute | solution.py:23
  127.5 3.2 fusion.39
  142.8 6.9 %broadcast_select_fusion.1 = (bf16[240,3072]{1,0:T(8,128)(2,1)}, bf16[240,3072]{1,0:T(8,128)(2,1)}, f32[240,3072]{1,0:T(8,128)S(1)}) fusion(pred[]{:T(512)S(6)} %eq.96, f32[240,3072]{1,0:T(8,128)S(1)} %copy-done.198, f32[240,3072]{1,0:T(8,128)S(1)} %copy-done.204, f32[3072]{0:T(1024)S(1)} %bitcast.412, ...), kind=kOutput, calls=%fused_computation.103 | convolution fusion | flops 1155502080 | bytes 17272704 | tf_op jit(solution)/shard_map/dot_general | solution.py:83
  153.3 4.3 fusion.65
  164.5 2.7 convolution_convert_fusion.6
  180.7 5.1 collective-permute-done.2
  188.9 5.2 fusion.58
  201.8 2.8 convolution_convert_fusion.3
  214.8 7.2 %collective-permute-done.3 = bf16[240,768]{1,0:T(8,128)(2,1)S(1)} collective-permute-done((bf16[240,768]{1,0:T(8,128)(2,1)S(1)}, bf16[240,768]{1,0:T(8,128)(2,1)S(1)}, u32[]{:S(2)}, u32[]{:S(2)}) %collective-permute-start.3) | collective-permute-done | bytes 368672 | tf_op jit(solution)/shard_map/ppermute | solution.py:23
  222.9 5.3 broadcast_select_fusion.3
  242.3 2.9 fusion.80
  251.4 2.7 fusion.79
  258.4 2.7 fusion.66
  267.0 2.9 collective-permute-done.20
  277.1 4.2 fusion.138
  307.2 3.3 all-reduce.2
  315.7 37.9 %all-reduce.3 = (f32[1,2,384]{2,1,0:T(2,128)}, f32[1,1536]{1,0:T(1,128)}, f32[1,2,384]{2,1,0:T(2,128)}, f32[1,2,384]{2,1,0:T(2,128)}, f32[1,2,384]{2,1,0:T(2,128)}) all-reduce(f32[1,2,384]{2,1,0:T(2,128)S(1)} %bitcast.413, f32[1,1536]{1,0:T(1,128)S(1)} %broadcast_in_dim.406, ...), channel_id=1, replica_groups=mesh['dp'=8,'pipe'=2,'pair'=2] {'dp'}, use_global_device_ids=true, to_apply=%region_35.36 | all-reduce | flops 4608 | bytes 36864 | tf_op jit(solution)/shard_map/psum | solution.py:411
  353.7 4.3 collective-permute-done.28
  358.0 4.3 collective-permute-done.29
  362.4 4.3 collective-permute-done.30
  366.8 4.3 collective-permute-done.31
  371.1 4.3 collective-permute-done.32
  376.7 5.9 %collective-permute-done.5 = bf16[48,2304]{1,0:T(8,128)(2,1)S(1)} collective-permute-done((bf16[48,2304]{1,0:T(8,128)(2,1)S(1)}, bf16[48,2304]{1,0:T(8,128)(2,1)S(1)}, u32[]{:S(2)}, u32[]{:S(2)}) %collective-permute-start.5) | collective-permute-done | bytes 221216 | tf_op jit(solution)/shard_map/ppermute | solution.py:259
  383.9 5.9 %collective-permute-done.6 = bf16[48,2304]{1,0:T(8,128)(2,1)S(1)} collective-permute-done((bf16[48,2304]{1,0:T(8,128)(2,1)S(1)}, bf16[48,2304]{1,0:T(8,128)(2,1)S(1)}, u32[]{:S(2)}, u32[]{:S(2)}) %collective-permute-start.6) | collective-permute-done | bytes 221216 | tf_op jit(solution)/shard_map/ppermute | solution.py:259
  401.5 4.2 collective-permute-done.8
  408.6 4.2 collective-permute-done.9
  438.0 8.1 %collective-permute-done.13 = bf16[48,2304]{1,0:T(8,128)(2,1)S(1)} collective-permute-done((bf16[48,2304]{1,0:T(8,128)(2,1)S(1)}, bf16[48,2304]{1,0:T(8,128)(2,1)S(1)}, u32[]{:S(2)}, u32[]{:S(2)}) %collective-permute-start.13) | collective-permute-done | bytes 221216 | tf_op jit(solution)/shard_map/ppermute | solution.py:279
  471.0 7.3 %collective-permute-done.17 = bf16[48,2304]{1,0:T(8,128)(2,1)S(1)} collective-permute-done((bf16[48,2304]{1,0:T(8,128)(2,1)S(1)}, bf16[48,2304]{1,0:T(8,128)(2,1)S(1)}, u32[]{:S(2)}, u32[]{:S(2)}) %collective-permute-start.17) | collective-permute-done | bytes 221216 | tf_op jit(solution)/shard_map/ppermute | solution.py:279
  484.3 3.1 collective-permute-done.43
  487.8 2.8 collective-permute-done.58
  491.0 3.2 collective-permute-done.44
  494.5 2.8 collective-permute-done.59
  497.7 3.2 collective-permute-done.45
  501.2 2.8 collective-permute-done.60
  504.4 3.2 collective-permute-done.46
  508.0 2.8 collective-permute-done.61
  511.1 3.2 collective-permute-done.47
  514.7 2.8 collective-permute-done.62
  517.9 3.2 collective-permute-done.48
  521.1 3.1 collective-permute-done.63
  (812 shorter events, 261.6 us)
Async XLA Ops:
  7.2 17.8 %all-gather.14.cloned.1.call-start = ((), (), s32[]{:S(2)}) async-start(), calls=%async_computation.4 | async-start | bytes 5308416 | tf_op jit(solution)/shard_map/all_gather | solution.py:325
  8.0 29.0 %all-gather.16.cloned.1.call-start = ((), (), s32[]{:S(2)}) async-start(), calls=%async_computation.5 | async-start | bytes 1769472 | tf_op jit(solution)/shard_map/all_gather | solution.py:326
  8.8 45.4 %all-gather.18.cloned.1.call-start = ((), (), s32[]{:S(2)}) async-start(), calls=%async_computation.6 | async-start | bytes 7077888 | tf_op jit(solution)/shard_map/all_gather | solution.py:327
  9.5 61.7 %all-gather.20.cloned.1.call-start = ((), (), s32[]{:S(2)}) async-start(), calls=%async_computation.7 | async-start | bytes 7077888 | tf_op jit(solution)/shard_map/all_gather | solution.py:328
  10.1 300.5 %reduce-scatter.13.cloned.1.call-start = ((), (), s32[]{:S(2)}) async-start(), calls=%async_computation.8 | async-start | bytes 589824
  77.6 12.1 %collective-permute-start = (bf16[240,768]{1,0:T(8,128)(2,1)S(1)}, bf16[240,768]{1,0:T(8,128)(2,1)S(1)}, u32[]{:S(2)}, u32[]{:S(2)}) collective-permute-start(bf16[240,768]{1,0:T(8,128)(2,1)S(1)} %add_convert_fusion.2), channel_id=1, source_target_pairs={{0,2},{1,3},{4,6},{5,7},{8,10},{9,11},{12,14},{13,15},{16,18},{17,... | collective-permute-start | bytes 1105928 | tf_op jit(solution)/shard_map/ppermute | solution.py:23
  111.1 14.6 %collective-permute-start.1 = (bf16[240,768]{1,0:T(8,128)(2,1)}, bf16[240,768]{1,0:T(8,128)(2,1)}, u32[]{:S(2)}, u32[]{:S(2)}) collective-permute-start(bf16[240,768]{1,0:T(8,128)(2,1)} %get-tuple-element.77), channel_id=1, source_target_pairs={{0,2},{1,3},{4,6},{5,7},{8,10},{9,11},{12,14},{13,15},{16,18},{17,... | collective-permute-start | bytes 1105928 | tf_op jit(solution)/shard_map/ppermute | solution.py:23
  173.9 11.9 %collective-permute-start.2 = (bf16[240,768]{1,0:T(8,128)(2,1)}, bf16[240,768]{1,0:T(8,128)(2,1)}, u32[]{:S(2)}, u32[]{:S(2)}) collective-permute-start(bf16[240,768]{1,0:T(8,128)(2,1)} %fusion.124), channel_id=1, source_target_pairs={{2,0},{3,1},{6,4},{7,5},{10,8},{11,9},{14,12},{15,13},{18,16},{19,... | collective-permute-start | bytes 1105928 | tf_op jit(solution)/shard_map/ppermute | solution.py:23
  211.2 10.8 %collective-permute-start.3 = (bf16[240,768]{1,0:T(8,128)(2,1)S(1)}, bf16[240,768]{1,0:T(8,128)(2,1)S(1)}, u32[]{:S(2)}, u32[]{:S(2)}) collective-permute-start(bf16[240,768]{1,0:T(8,128)(2,1)S(1)} %get-tuple-element.122), channel_id=1, source_target_pairs={{2,0},{3,1},{6,4},{7,5},{10,8},{11,9},{14,12},{15,13},{18,16},{19,... | collective-permute-start | bytes 1105928 | tf_op jit(solution)/shard_map/ppermute | solution.py:23
  246.6 128.8 %collective-permute-start.4 = (bf16[384,2304]{1,0:T(8,128)(2,1)}, bf16[384,2304]{1,0:T(8,128)(2,1)}, u32[]{:S(2)}, u32[]{:S(2)}) collective-permute-start(bf16[384,2304]{1,0:T(8,128)(2,1)} %dynamic-slice_convert_fusion.2), channel_id=1, source_target_pairs={{0,1},{1,0},{2,3},{3,2},{4,5},{5,4},{6,7},{7,6},{8,9},{9,8},{10,11... | collective-permute-start | bytes 5308424 | tf_op jit(solution)/shard_map/ppermute | solution.py:304
  249.2 16.2 %collective-permute-start.19 = (bf16[384,768]{1,0:T(8,128)(2,1)S(1)}, bf16[384,768]{1,0:T(8,128)(2,1)S(1)}, u32[]{:S(2)}, u32[]{:S(2)}) collective-permute-start(bf16[384,768]{1,0:T(8,128)(2,1)S(1)} %dynamic-slice_convert_fusion.3), channel_id=1, source_target_pairs={{0,1},{1,0},{2,3},{3,2},{4,5},{5,4},{6,7},{7,6},{8,9},{9,8},{10,11... | collective-permute-start | bytes 1769480 | tf_op jit(solution)/shard_map/ppermute | solution.py:304
  255.9 135.2 %collective-permute-start.34 = (bf16[384,3072]{1,0:T(8,128)(2,1)}, bf16[384,3072]{1,0:T(8,128)(2,1)}, u32[]{:S(2)}, u32[]{:S(2)}) collective-permute-start(bf16[384,3072]{1,0:T(8,128)(2,1)} %dynamic-slice_convert_fusion.1), channel_id=1, source_target_pairs={{0,1},{1,0},{2,3},{3,2},{4,5},{5,4},{6,7},{7,6},{8,9},{9,8},{10,11... | collective-permute-start | bytes 7077896 | tf_op jit(solution)/shard_map/ppermute | solution.py:304
  263.0 129.4 %collective-permute-start.49 = (bf16[1536,768]{1,0:T(8,128)(2,1)}, bf16[1536,768]{1,0:T(8,128)(2,1)}, u32[]{:S(2)}, u32[]{:S(2)}) collective-permute-start(bf16[1536,768]{1,0:T(8,128)(2,1)} %dynamic-slice_convert_fusion), channel_id=1, source_target_pairs={{0,1},{1,0},{2,3},{3,2},{4,5},{5,4},{6,7},{7,6},{8,9},{9,8},{10,11... | collective-permute-start | bytes 7077896 | tf_op jit(solution)/shard_map/ppermute | solution.py:304
  272.4 39.2 %reduce-scatter.15.cloned.1.call-start = ((), (), s32[]{:S(2)}) async-start(), calls=%async_computation.9 | async-start | bytes 589824
  285.5 27.1 %reduce-scatter.17.cloned.1.call-start = ((), (), s32[]{:S(2)}) async-start(), calls=%async_computation.10 | async-start | bytes 589824
  290.9 23.8 %reduce-scatter.19.cloned.1.call-start = ((), (), s32[]{:S(2)}) async-start(), calls=%async_computation.11 | async-start | bytes 589824
  304.6 49.1 %collective-permute-start.27 = (bf16[48,768]{1,0:T(8,128)(2,1)S(1)}, bf16[48,768]{1,0:T(8,128)(2,1)S(1)}, u32[]{:S(2)}, u32[]{:S(2)}) collective-permute-start(bf16[48,768]{1,0:T(8,128)(2,1)S(1)} %get-tuple-element.53), channel_id=1, source_target_pairs={{0,8},{9,1},{4,0},{1,5},{8,16},{17,9},{12,4},{5,13},{16,24},{25,17... | collective-permute-start | bytes 221192 | tf_op jit(solution)/shard_map/ppermute | solution.py:279
  375.4 8.4 %collective-permute-start.33 = (bf16[48,768]{1,0:T(8,128)(2,1)S(1)}, bf16[48,768]{1,0:T(8,128)(2,1)S(1)}, u32[]{:S(2)}, u32[]{:S(2)}) collective-permute-start(bf16[48,768]{1,0:T(8,128)(2,1)S(1)} %collective-permute-done.32), channel_id=1, source_target_pairs={{0,8},{9,1},{4,0},{1,5},{8,16},{17,9},{12,4},{5,13},{16,24},{25,17... | collective-permute-start | bytes 221192 | tf_op jit(solution)/shard_map/ppermute | solution.py:279
  392.3 7.8 %collective-permute-start.35 = (bf16[48,3072]{1,0:T(8,128)(2,1)S(1)}, bf16[48,3072]{1,0:T(8,128)(2,1)S(1)}, u32[]{:S(2)}, u32[]{:S(2)}) collective-permute-start(bf16[48,3072]{1,0:T(8,128)(2,1)S(1)} %add_convert_fusion.24), channel_id=1, source_target_pairs={{0,8},{9,1},{4,0},{1,5},{8,16},{17,9},{12,4},{5,13},{16,24},{25,17... | collective-permute-start | bytes 884744 | tf_op jit(solution)/shard_map/ppermute | solution.py:259
  393.7 13.3 %collective-permute-start.50 = (bf16[192,768]{1,0:T(8,128)(2,1)S(1)}, bf16[192,768]{1,0:T(8,128)(2,1)S(1)}, u32[]{:S(2)}, u32[]{:S(2)}) collective-permute-start(bf16[192,768]{1,0:T(8,128)(2,1)S(1)} %add_convert_fusion.16), channel_id=1, source_target_pairs={{0,8},{9,1},{4,0},{1,5},{8,16},{17,9},{12,4},{5,13},{16,24},{25,17... | collective-permute-start | bytes 884744 | tf_op jit(solution)/shard_map/ppermute | solution.py:259
  398.2 7.5 %collective-permute-start.8 = (bf16[48,2304]{1,0:T(8,128)(2,1)S(1)}, bf16[48,2304]{1,0:T(8,128)(2,1)S(1)}, u32[]{:S(2)}, u32[]{:S(2)}) collective-permute-start(bf16[48,2304]{1,0:T(8,128)(2,1)S(1)} %add_convert_fusion.29), channel_id=1, source_target_pairs={{0,8},{9,1},{4,0},{1,5},{8,16},{17,9},{12,4},{5,13},{16,24},{25,17... | collective-permute-start | bytes 663560 | tf_op jit(solution)/shard_map/ppermute | solution.py:259
  401.4 12.7 %collective-permute-start.36 = (bf16[48,3072]{1,0:T(8,128)(2,1)S(1)}, bf16[48,3072]{1,0:T(8,128)(2,1)S(1)}, u32[]{:S(2)}, u32[]{:S(2)}) collective-permute-start(bf16[48,3072]{1,0:T(8,128)(2,1)S(1)} %add_convert_fusion.23), channel_id=1, source_target_pairs={{0,8},{9,1},{4,0},{1,5},{8,16},{17,9},{12,4},{5,13},{16,24},{25,17... | collective-permute-start | bytes 884744 | tf_op jit(solution)/shard_map/ppermute | solution.py:259
  408.2 7.8 %collective-permute-start.51 = (bf16[192,768]{1,0:T(8,128)(2,1)S(1)}, bf16[192,768]{1,0:T(8,128)(2,1)S(1)}, u32[]{:S(2)}, u32[]{:S(2)}) collective-permute-start(bf16[192,768]{1,0:T(8,128)(2,1)S(1)} %add_convert_fusion.15), channel_id=1, source_target_pairs={{0,8},{9,1},{4,0},{1,5},{8,16},{17,9},{12,4},{5,13},{16,24},{25,17... | collective-permute-start | bytes 884744 | tf_op jit(solution)/shard_map/ppermute | solution.py:259
  415.4 7.8 %collective-permute-start.37 = (bf16[48,3072]{1,0:T(8,128)(2,1)S(1)}, bf16[48,3072]{1,0:T(8,128)(2,1)S(1)}, u32[]{:S(2)}, u32[]{:S(2)}) collective-permute-start(bf16[48,3072]{1,0:T(8,128)(2,1)S(1)} %add_convert_fusion.22), channel_id=1, source_target_pairs={{0,8},{9,1},{4,0},{1,5},{8,16},{17,9},{12,4},{5,13},{16,24},{25,17... | collective-permute-start | bytes 884744 | tf_op jit(solution)/shard_map/ppermute | solution.py:259
  417.3 9.1 %collective-permute-start.52 = (bf16[192,768]{1,0:T(8,128)(2,1)S(1)}, bf16[192,768]{1,0:T(8,128)(2,1)S(1)}, u32[]{:S(2)}, u32[]{:S(2)}) collective-permute-start(bf16[192,768]{1,0:T(8,128)(2,1)S(1)} %add_convert_fusion.14), channel_id=1, source_target_pairs={{0,8},{9,1},{4,0},{1,5},{8,16},{17,9},{12,4},{5,13},{16,24},{25,17... | collective-permute-start | bytes 884744 | tf_op jit(solution)/shard_map/ppermute | solution.py:259
  421.2 7.5 %collective-permute-start.11 = (bf16[48,2304]{1,0:T(8,128)(2,1)S(1)}, bf16[48,2304]{1,0:T(8,128)(2,1)S(1)}, u32[]{:S(2)}, u32[]{:S(2)}) collective-permute-start(bf16[48,2304]{1,0:T(8,128)(2,1)S(1)} %add_convert_fusion.26), channel_id=1, source_target_pairs={{0,8},{9,1},{4,0},{1,5},{8,16},{17,9},{12,4},{5,13},{16,24},{25,17... | collective-permute-start | bytes 663560 | tf_op jit(solution)/shard_map/ppermute | solution.py:259
  424.5 7.4 %collective-permute-start.38 = (bf16[48,3072]{1,0:T(8,128)(2,1)S(1)}, bf16[48,3072]{1,0:T(8,128)(2,1)S(1)}, u32[]{:S(2)}, u32[]{:S(2)}) collective-permute-start(bf16[48,3072]{1,0:T(8,128)(2,1)S(1)} %add_convert_fusion.21), channel_id=1, source_target_pairs={{0,8},{9,1},{4,0},{1,5},{8,16},{17,9},{12,4},{5,13},{16,24},{25,17... | collective-permute-start | bytes 884744 | tf_op jit(solution)/shard_map/ppermute | solution.py:259
  427.6 7.4 %collective-permute-start.53 = (bf16[192,768]{1,0:T(8,128)(2,1)S(1)}, bf16[192,768]{1,0:T(8,128)(2,1)S(1)}, u32[]{:S(2)}, u32[]{:S(2)}) collective-permute-start(bf16[192,768]{1,0:T(8,128)(2,1)S(1)} %add_convert_fusion.13), channel_id=1, source_target_pairs={{0,8},{9,1},{4,0},{1,5},{8,16},{17,9},{12,4},{5,13},{16,24},{25,17... | collective-permute-start | bytes 884744 | tf_op jit(solution)/shard_map/ppermute | solution.py:259
  430.2 7.2 %collective-permute-start.12 = (bf16[48,2304]{1,0:T(8,128)(2,1)S(1)}, bf16[48,2304]{1,0:T(8,128)(2,1)S(1)}, u32[]{:S(2)}, u32[]{:S(2)}) collective-permute-start(bf16[48,2304]{1,0:T(8,128)(2,1)S(1)} %get-tuple-element.57), channel_id=1, source_target_pairs={{0,8},{9,1},{4,0},{1,5},{8,16},{17,9},{12,4},{5,13},{16,24},{25,17... | collective-permute-start | bytes 663560 | tf_op jit(solution)/shard_map/ppermute | solution.py:279
  433.2 13.0 %collective-permute-start.39 = (bf16[48,3072]{1,0:T(8,128)(2,1)S(1)}, bf16[48,3072]{1,0:T(8,128)(2,1)S(1)}, u32[]{:S(2)}, u32[]{:S(2)}) collective-permute-start(bf16[48,3072]{1,0:T(8,128)(2,1)S(1)} %add_convert_fusion.20), channel_id=1, source_target_pairs={{0,8},{9,1},{4,0},{1,5},{8,16},{17,9},{12,4},{5,13},{16,24},{25,17... | collective-permute-start | bytes 884744 | tf_op jit(solution)/shard_map/ppermute | solution.py:259
  436.3 12.5 %collective-permute-start.54 = (bf16[192,768]{1,0:T(8,128)(2,1)S(1)}, bf16[192,768]{1,0:T(8,128)(2,1)S(1)}, u32[]{:S(2)}, u32[]{:S(2)}) collective-permute-start(bf16[192,768]{1,0:T(8,128)(2,1)S(1)} %add_convert_fusion.12), channel_id=1, source_target_pairs={{0,8},{9,1},{4,0},{1,5},{8,16},{17,9},{12,4},{5,13},{16,24},{25,17... | collective-permute-start | bytes 884744 | tf_op jit(solution)/shard_map/ppermute | solution.py:259
  437.4 8.7 %collective-permute-start.13 = (bf16[48,2304]{1,0:T(8,128)(2,1)S(1)}, bf16[48,2304]{1,0:T(8,128)(2,1)S(1)}, u32[]{:S(2)}, u32[]{:S(2)}) collective-permute-start(bf16[48,2304]{1,0:T(8,128)(2,1)S(1)} %collective-permute-done.12), channel_id=1, source_target_pairs={{0,8},{9,1},{4,0},{1,5},{8,16},{17,9},{12,4},{5,13},{16,24},{25,17... | collective-permute-start | bytes 663560 | tf_op jit(solution)/shard_map/ppermute | solution.py:279
  447.5 7.7 %collective-permute-start.40 = (bf16[48,3072]{1,0:T(8,128)(2,1)S(1)}, bf16[48,3072]{1,0:T(8,128)(2,1)S(1)}, u32[]{:S(2)}, u32[]{:S(2)}) collective-permute-start(bf16[48,3072]{1,0:T(8,128)(2,1)S(1)} %add_convert_fusion.19), channel_id=1, source_target_pairs={{0,8},{9,1},{4,0},{1,5},{8,16},{17,9},{12,4},{5,13},{16,24},{25,17... | collective-permute-start | bytes 884744 | tf_op jit(solution)/shard_map/ppermute | solution.py:259
  450.1 8.3 %collective-permute-start.55 = (bf16[192,768]{1,0:T(8,128)(2,1)S(1)}, bf16[192,768]{1,0:T(8,128)(2,1)S(1)}, u32[]{:S(2)}, u32[]{:S(2)}) collective-permute-start(bf16[192,768]{1,0:T(8,128)(2,1)S(1)} %add_convert_fusion.11), channel_id=1, source_target_pairs={{0,8},{9,1},{4,0},{1,5},{8,16},{17,9},{12,4},{5,13},{16,24},{25,17... | collective-permute-start | bytes 884744 | tf_op jit(solution)/shard_map/ppermute | solution.py:259
  452.0 8.7 %collective-permute-start.15 = (bf16[48,2304]{1,0:T(8,128)(2,1)S(1)}, bf16[48,2304]{1,0:T(8,128)(2,1)S(1)}, u32[]{:S(2)}, u32[]{:S(2)}) collective-permute-start(bf16[48,2304]{1,0:T(8,128)(2,1)S(1)} %collective-permute-done.14), channel_id=1, source_target_pairs={{0,8},{9,1},{4,0},{1,5},{8,16},{17,9},{12,4},{5,13},{16,24},{25,17... | collective-permute-start | bytes 663560 | tf_op jit(solution)/shard_map/ppermute | solution.py:279
  456.5 7.4 %collective-permute-start.41 = (bf16[48,3072]{1,0:T(8,128)(2,1)S(1)}, bf16[48,3072]{1,0:T(8,128)(2,1)S(1)}, u32[]{:S(2)}, u32[]{:S(2)}) collective-permute-start(bf16[48,3072]{1,0:T(8,128)(2,1)S(1)} %add_convert_fusion.18), channel_id=1, source_target_pairs={{0,8},{9,1},{4,0},{1,5},{8,16},{17,9},{12,4},{5,13},{16,24},{25,17... | collective-permute-start | bytes 884744 | tf_op jit(solution)/shard_map/ppermute | solution.py:259
  459.6 7.4 %collective-permute-start.56 = (bf16[192,768]{1,0:T(8,128)(2,1)S(1)}, bf16[192,768]{1,0:T(8,128)(2,1)S(1)}, u32[]{:S(2)}, u32[]{:S(2)}) collective-permute-start(bf16[192,768]{1,0:T(8,128)(2,1)S(1)} %add_convert_fusion.10), channel_id=1, source_target_pairs={{0,8},{9,1},{4,0},{1,5},{8,16},{17,9},{12,4},{5,13},{16,24},{25,17... | collective-permute-start | bytes 884744 | tf_op jit(solution)/shard_map/ppermute | solution.py:259
  460.7 8.8 %collective-permute-start.16 = (bf16[48,2304]{1,0:T(8,128)(2,1)S(1)}, bf16[48,2304]{1,0:T(8,128)(2,1)S(1)}, u32[]{:S(2)}, u32[]{:S(2)}) collective-permute-start(bf16[48,2304]{1,0:T(8,128)(2,1)S(1)} %collective-permute-done.15), channel_id=1, source_target_pairs={{0,8},{9,1},{4,0},{1,5},{8,16},{17,9},{12,4},{5,13},{16,24},{25,17... | collective-permute-start | bytes 663560 | tf_op jit(solution)/shard_map/ppermute | solution.py:279
  465.8 12.9 %collective-permute-start.42 = (bf16[48,3072]{1,0:T(8,128)(2,1)S(1)}, bf16[48,3072]{1,0:T(8,128)(2,1)S(1)}, u32[]{:S(2)}, u32[]{:S(2)}) collective-permute-start(bf16[48,3072]{1,0:T(8,128)(2,1)S(1)} %get-tuple-element.49), channel_id=1, source_target_pairs={{0,8},{9,1},{4,0},{1,5},{8,16},{17,9},{12,4},{5,13},{16,24},{25,17... | collective-permute-start | bytes 884744 | tf_op jit(solution)/shard_map/ppermute | solution.py:279
  468.7 11.6 %collective-permute-start.57 = (bf16[192,768]{1,0:T(8,128)(2,1)S(1)}, bf16[192,768]{1,0:T(8,128)(2,1)S(1)}, u32[]{:S(2)}, u32[]{:S(2)}) collective-permute-start(bf16[192,768]{1,0:T(8,128)(2,1)S(1)} %get-tuple-element.45), channel_id=1, source_target_pairs={{0,8},{9,1},{4,0},{1,5},{8,16},{17,9},{12,4},{5,13},{16,24},{25,17... | collective-permute-start | bytes 884744 | tf_op jit(solution)/shard_map/ppermute | solution.py:279
  469.6 8.7 %collective-permute-start.17 = (bf16[48,2304]{1,0:T(8,128)(2,1)S(1)}, bf16[48,2304]{1,0:T(8,128)(2,1)S(1)}, u32[]{:S(2)}, u32[]{:S(2)}) collective-permute-start(bf16[48,2304]{1,0:T(8,128)(2,1)S(1)} %collective-permute-done.16), channel_id=1, source_target_pairs={{0,8},{9,1},{4,0},{1,5},{8,16},{17,9},{12,4},{5,13},{16,24},{25,17... | collective-permute-start | bytes 663560 | tf_op jit(solution)/shard_map/ppermute | solution.py:279
  478.7 8.7 %collective-permute-start.43 = (bf16[48,3072]{1,0:T(8,128)(2,1)S(1)}, bf16[48,3072]{1,0:T(8,128)(2,1)S(1)}, u32[]{:S(2)}, u32[]{:S(2)}) collective-permute-start(bf16[48,3072]{1,0:T(8,128)(2,1)S(1)} %collective-permute-done.42), channel_id=1, source_target_pairs={{0,8},{9,1},{4,0},{1,5},{8,16},{17,9},{12,4},{5,13},{16,24},{25,17... | collective-permute-start | bytes 884744 | tf_op jit(solution)/shard_map/ppermute | solution.py:279
  480.3 10.3 %collective-permute-start.58 = (bf16[192,768]{1,0:T(8,128)(2,1)S(1)}, bf16[192,768]{1,0:T(8,128)(2,1)S(1)}, u32[]{:S(2)}, u32[]{:S(2)}) collective-permute-start(bf16[192,768]{1,0:T(8,128)(2,1)S(1)} %collective-permute-done.57), channel_id=1, source_target_pairs={{0,8},{9,1},{4,0},{1,5},{8,16},{17,9},{12,4},{5,13},{16,24},{25,17... | collective-permute-start | bytes 884744 | tf_op jit(solution)/shard_map/ppermute | solution.py:279
  487.4 6.7 %collective-permute-start.44 = (bf16[48,3072]{1,0:T(8,128)(2,1)S(1)}, bf16[48,3072]{1,0:T(8,128)(2,1)S(1)}, u32[]{:S(2)}, u32[]{:S(2)}) collective-permute-start(bf16[48,3072]{1,0:T(8,128)(2,1)S(1)} %collective-permute-done.43), channel_id=1, source_target_pairs={{0,8},{9,1},{4,0},{1,5},{8,16},{17,9},{12,4},{5,13},{16,24},{25,17... | collective-permute-start | bytes 884744 | tf_op jit(solution)/shard_map/ppermute | solution.py:279
  490.6 6.7 %collective-permute-start.59 = (bf16[192,768]{1,0:T(8,128)(2,1)S(1)}, bf16[192,768]{1,0:T(8,128)(2,1)S(1)}, u32[]{:S(2)}, u32[]{:S(2)}) collective-permute-start(bf16[192,768]{1,0:T(8,128)(2,1)S(1)} %collective-permute-done.58), channel_id=1, source_target_pairs={{0,8},{9,1},{4,0},{1,5},{8,16},{17,9},{12,4},{5,13},{16,24},{25,17... | collective-permute-start | bytes 884744 | tf_op jit(solution)/shard_map/ppermute | solution.py:279
  494.1 6.7 %collective-permute-start.45 = (bf16[48,3072]{1,0:T(8,128)(2,1)S(1)}, bf16[48,3072]{1,0:T(8,128)(2,1)S(1)}, u32[]{:S(2)}, u32[]{:S(2)}) collective-permute-start(bf16[48,3072]{1,0:T(8,128)(2,1)S(1)} %collective-permute-done.44), channel_id=1, source_target_pairs={{0,8},{9,1},{4,0},{1,5},{8,16},{17,9},{12,4},{5,13},{16,24},{25,17... | collective-permute-start | bytes 884744 | tf_op jit(solution)/shard_map/ppermute | solution.py:279
  497.3 6.7 %collective-permute-start.60 = (bf16[192,768]{1,0:T(8,128)(2,1)S(1)}, bf16[192,768]{1,0:T(8,128)(2,1)S(1)}, u32[]{:S(2)}, u32[]{:S(2)}) collective-permute-start(bf16[192,768]{1,0:T(8,128)(2,1)S(1)} %collective-permute-done.59), channel_id=1, source_target_pairs={{0,8},{9,1},{4,0},{1,5},{8,16},{17,9},{12,4},{5,13},{16,24},{25,17... | collective-permute-start | bytes 884744 | tf_op jit(solution)/shard_map/ppermute | solution.py:279
  500.9 6.7 %collective-permute-start.46 = (bf16[48,3072]{1,0:T(8,128)(2,1)S(1)}, bf16[48,3072]{1,0:T(8,128)(2,1)S(1)}, u32[]{:S(2)}, u32[]{:S(2)}) collective-permute-start(bf16[48,3072]{1,0:T(8,128)(2,1)S(1)} %collective-permute-done.45), channel_id=1, source_target_pairs={{0,8},{9,1},{4,0},{1,5},{8,16},{17,9},{12,4},{5,13},{16,24},{25,17... | collective-permute-start | bytes 884744 | tf_op jit(solution)/shard_map/ppermute | solution.py:279
  (246 other events, 1504.8 us)
Sparse Core Ops, SparseCore 0:
  9.6 15.3 all-gather.13
  26.5 10.3 all-gather.15
  38.5 15.5 all-gather.17
  55.6 15.6 all-gather.19
  272.5 6.8 reduce-scatter.12
  285.6 5.9 reduce-scatter.14
  293.9 8.9 reduce-scatter.16
  307.3 7.3 reduce-scatter.18
